TPU v7x, 512 devices: a whole 4x4x16 slice. The times are simulated.
512 devices in a mesh: row: 16 (over z_lo, y), col: 32 (over z_hi, x, core).
Axes of the slice: x: 4, y: 4, z: 16 (z_hi: 4, z_lo: 4; z = z_hi * 4 + z_lo), core: 2. Of those that a mesh axis runs over, the one named last changes fastest.
Arguments:
- contact_map: bfloat16 [1024, 1024, 128], P('row', 'col'), may hold values from -6 to 6
- cotangent: bfloat16 [1024, 1024, 128], P('row', 'col'), may hold values from -6 to 6
- conv_weight: bfloat16 [3, 3, 3, 128, 128], replicated, may hold values from -0.1875 to 0.1875
- proj_weight: bfloat16 [3, 128, 128], replicated, may hold values from -0.5 to 0.5
Outputs:
- map_grad: bfloat16 [1024, 1024, 128], P('row', 'col')
- conv_grad: float32 [3, 3, 3, 128, 128], replicated
- proj_grad: float32 [3, 128, 128], replicated
All inputs are finite; a program needn't handle non-finite values.
Results may differ from a plain program's by a relative error of at most 0.019.
Values may be sent and summed in bfloat16 or wider, within the bound.
A program may use at most 64 MiB of HBM per device.

v0:
```python
import jax
import jax.numpy as jnp
from jax import lax
from jax.sharding import PartitionSpec as P


def with_halo(cells, sides, width):
    for axis, dim in sides:
        count = lax.axis_size(axis)
        ends = count - 1
        head = lax.slice_in_dim(cells, 0, width, axis=dim)
        tail = lax.slice_in_dim(cells, cells.shape[dim] - width, cells.shape[dim], axis=dim)
        cells = jnp.concatenate(
            [
                lax.ppermute(tail, axis, [(i, (i + 1) % count) for i in range(ends)]),
                cells,
                lax.ppermute(head, axis, [((i + 1) % count, i) for i in range(ends)]),
            ],
            axis=dim,
        )
    return cells


def gelu_slope(values):
    return jax.vjp(jax.nn.gelu, values)[1](jnp.ones_like(values))[0]


def dilated_valid(widened, kernel, dilation):
    return lax.conv_general_dilated(
        widened[None],
        kernel,
        (1, 1),
        "VALID",
        rhs_dilation=(dilation, dilation),
        dimension_numbers=("NHWC", "HWIO", "NHWC"),
        preferred_element_type=jnp.float32,
    )[0]


def mirror(local_tile):
    tile_rows, tile_cols, channels = local_tile.shape
    col_count = lax.axis_size("col")
    row_ratio = tile_rows // tile_cols
    strips = tile_cols // col_count
    sectioned = local_tile.reshape(row_ratio, col_count, strips, tile_cols, channels)
    sectioned = sectioned.transpose(1, 0, 2, 3, 4).reshape(tile_rows, tile_cols, channels)
    sectioned = lax.all_to_all(sectioned, "col", split_axis=0, concat_axis=1, tiled=True)
    sectioned = lax.all_to_all(
        lax.all_to_all(sectioned, "row", split_axis=1, concat_axis=0, tiled=True),
        "col",
        split_axis=0,
        concat_axis=0,
        tiled=True,
    )
    return sectioned.transpose(1, 0, 2)


def body(contact_map, cotangent, conv_weight, proj_weight):
    tile_rows, tile_cols, channels = contact_map.shape
    map_bins = tile_cols * lax.axis_size("col")
    block_count = conv_weight.shape[0]
    contract_rows = (((0,), (0,)), ((), ()))
    contract_cols = (((1,), (1,)), ((), ()))
    hidden = (
        0.5 * (contact_map.astype(jnp.float32) + mirror(contact_map).astype(jnp.float32))
    ).astype(jnp.bfloat16)
    stored = []
    for block_index in range(block_count):
        dilation = 2 ** (block_index + 1)
        activated = jax.nn.gelu(hidden.astype(jnp.float32)).astype(jnp.bfloat16)
        widened = with_halo(activated, (("row", 0), ("col", 1)), dilation)
        summed = dilated_valid(widened, conv_weight[block_index], dilation)
        middle = jax.nn.gelu(summed).astype(jnp.bfloat16)
        stored.append((hidden, widened, summed, middle))
        if block_index + 1 < block_count:
            branch = jnp.dot(
                middle.reshape(-1, channels),
                proj_weight[block_index],
                preferred_element_type=jnp.float32,
            )
            hidden = (
                hidden.astype(jnp.float32) + branch.reshape(tile_rows, tile_cols, channels)
            ).astype(jnp.bfloat16)
    gradient = cotangent
    conv_terms = []
    proj_terms = []
    for block_index in reversed(range(block_count)):
        dilation = 2 ** (block_index + 1)
        hidden, widened, summed, middle = stored[block_index]
        flat_grad = gradient.reshape(-1, channels)
        back_middle = lax.dot_general(
            flat_grad, proj_weight[block_index], contract_cols, preferred_element_type=jnp.float32
        )
        back_summed = (
            back_middle.reshape(tile_rows, tile_cols, channels) * gelu_slope(summed)
        ).astype(jnp.bfloat16)
        back_wide = with_halo(back_summed, (("row", 0), ("col", 1)), dilation)
        proj_term = lax.dot_general(
            middle.reshape(-1, channels),
            flat_grad,
            contract_rows,
            preferred_element_type=jnp.float32,
        )
        flat_back = back_summed.reshape(-1, channels)
        tap_terms = []
        for tap_row in range(3):
            for tap_col in range(3):
                window = widened[
                    tap_row * dilation : tap_row * dilation + tile_rows,
                    tap_col * dilation : tap_col * dilation + tile_cols,
                ]
                tap_terms.append(
                    lax.dot_general(
                        window.reshape(-1, channels),
                        flat_back,
                        contract_rows,
                        preferred_element_type=jnp.float32,
                    )
                )
        conv_term = jnp.stack(tap_terms).reshape(3, 3, channels, channels)
        flipped_kernel = jnp.swapaxes(conv_weight[block_index][::-1, ::-1], 2, 3)
        back_act = dilated_valid(back_wide, flipped_kernel, dilation)
        gradient = (
            gradient.astype(jnp.float32) + back_act * gelu_slope(hidden.astype(jnp.float32))
        ).astype(jnp.bfloat16)
        conv_terms.append(conv_term)
        proj_terms.append(proj_term)
    conv_stack = jnp.stack(conv_terms[::-1])
    proj_stack = jnp.stack(proj_terms[::-1])
    conv_stack, proj_stack = lax.psum((conv_stack, proj_stack), ("row", "col"))
    map_grad = (0.5 * (gradient.astype(jnp.float32) + mirror(gradient).astype(jnp.float32))).astype(
        jnp.bfloat16
    )
    return (map_grad, conv_stack / map_bins, proj_stack / map_bins)


def solution(mesh):
    in_specs = (P("row", "col", None), P("row", "col", None), P(), P())
    out_specs = (P("row", "col", None), P(), P())
    return jax.shard_map(body, mesh=mesh, in_specs=in_specs, out_specs=out_specs, check_vma=False)
```

profile of v0, /device:TPU:1, one launch (start us, length us, event | category | flops | bytes accessed | tf_op | source)
XLA Modules:
  0.0 867.4 jit_solution(18233996569170081543)
XLA Ops:
  8.3 48.3 %all_to_all.82 = bf16[64,32,128]{2,1,0:T(8,128)(2,1)S(1)} all-to-all(bf16[64,32,128]{2,1,0:T(8,128)(2,1)S(1)} %bitcast.333), channel_id=1, replica_groups=mesh['row'=16,'col'=32] {'col'}, dimensions={0} | all-to-all | bytes 1048576 | tf_op jit(solution)/shard_map/all_to_all | solution.py:47
  57.1 25.2 %all_to_all.83 = bf16[2,1024,128]{2,0,1:T(2,128)(2,1)S(1)} all-to-all(bf16[2,1024,128]{2,0,1:T(2,128)(2,1)S(1)} %copy.236), channel_id=1, replica_groups=mesh['row'=16,'col'=32] {'row'}, dimensions={1} | all-to-all | bytes 1048576 | tf_op jit(solution)/shard_map/all_to_all | solution.py:49
  82.5 27.6 %all_to_all.84 = bf16[32,64,128]{2,1,0:T(8,128)(2,1)S(1)} all-to-all(bf16[32,64,128]{2,1,0:T(8,128)(2,1)S(1)} %bitcast.330), channel_id=1, replica_groups=mesh['row'=16,'col'=32] {'col'}, dimensions={0} | all-to-all | bytes 1048576 | tf_op jit(solution)/shard_map/all_to_all | solution.py:48
  110.7 2.8 collective-permute-start
  114.8 8.6 collective-permute-done.1
  123.5 3.3 collective-permute-start.2
  126.8 1.9 collective-permute-start.3
  128.7 3.3 collective-permute-done.3
  133.8 2.0 fusion.20
  137.7 3.6 collective-permute-start.4
  142.6 7.5 collective-permute-done.5
  150.2 3.1 collective-permute-start.6
  153.3 2.5 collective-permute-start.7
  155.8 3.1 collective-permute-done.7
  159.3 4.6 fusion.11
  164.7 5.7 collective-permute-start.8
  171.8 4.0 collective-permute-done.9
  175.8 3.0 collective-permute-start.10
  178.8 2.1 collective-permute-start.11
  180.9 1.5 pad_maximum_fusion.3
  185.6 4.9 fusion.4
  191.8 3.7 collective-permute-start.12
  200.9 3.5 collective-permute-start.14
  204.4 2.1 collective-permute-start.15
  206.9 5.5 collective-permute-done.15
  212.5 4.9 fusion.2
  219.1 4.0 collective-permute-start.16
  224.7 3.0 collective-permute-done.17
  227.8 3.2 collective-permute-start.18
  231.0 2.2 collective-permute-start.19
  233.5 9.1 %collective-permute-done.19 = bf16[72,4,128]{2,1,0:T(4,128)(2,1)S(1)} collective-permute-done((bf16[72,4,128]{2,1,0:T(4,128)(2,1)S(1)}, bf16[72,4,128]{2,1,0:T(4,128)(2,1)S(1)}, u32[]{:S(2)}, u32[]{:S(2)}) %collective-permute-start.19) | collective-permute-done | bytes 73760 | tf_op jit(solution)/shard_map/ppermute | solution.py:17
  243.0 4.6 fusion.9
  249.7 4.0 collective-permute-start.20
  256.0 2.2 collective-permute-done.21
  258.2 3.3 collective-permute-start.22
  261.5 2.4 collective-permute-start.23
  264.9 8.6 collective-permute-done.23
  274.3 1.8 convolution_select_fusion
  278.6 33.9 %all-to-all-start.3 = ((bf16[64,32,128]{2,1,0:T(8,128)(2,1)}), bf16[64,32,128]{2,1,0:T(8,128)(2,1)}, u32[]{:S(2)}, u32[]{:S(2)}) async-start(bf16[64,32,128]{2,1,0:T(8,128)(2,1)} %bitcast.326), calls=%async_computation.3 | async-start | bytes 1048576 | tf_op jit(solution)/shard_map/all_to_all | solution.py:47
  312.5 2.1 fusion.56
  323.1 17.2 %all-to-all-done.3 = bf16[64,32,128]{2,1,0:T(8,128)(2,1)} async-done(((bf16[64,32,128]{2,1,0:T(8,128)(2,1)}), bf16[64,32,128]{2,1,0:T(8,128)(2,1)}, u32[]{:S(2)}, u32[]{:S(2)}) %all-to-all-start.3) | async-done | bytes 524320 | tf_op jit(solution)/shard_map/all_to_all | solution.py:47
  342.7 5.6 all-to-all-start.4
  356.6 5.3 all-to-all-done.4
  362.9 9.9 %all-to-all-start.5 = ((bf16[32,64,128]{2,1,0:T(8,128)(2,1)}), bf16[32,64,128]{2,1,0:T(8,128)(2,1)S(1)}, u32[]{:S(2)}, u32[]{:S(2)}) async-start(bf16[32,64,128]{2,1,0:T(8,128)(2,1)} %bitcast.53), calls=%async_computation.5 | async-start | bytes 1048576 | tf_op jit(solution)/shard_map/all_to_all | solution.py:48
  374.6 2.4 pad_maximum_fusion
  377.0 477.7 %all-reduce.3.cloned.1.call-done = (f32[3,3,3,128,128]{4,3,2,1,0:T(8,128)}, f32[3,128,128]{2,1,0:T(8,128)}) async-done(((f32[3,3,3,128,128]{4,3,2,1,0:T(8,128)}, f32[3,128,128]{2,1,0:T(8,128)}), (f32[3,3,3,128,128]{4,3,2,1,0:T(8,128)}, f32[3,128,128]{2,1,0:T(8,128)})) %all-reduce.3.cloned.1.call-update) | async-done | bytes 1966096 | tf_op jit(solution)/shard_map/psum | solution.py:130
  854.7 1.6 broadcast_multiply_fusion.1
  856.3 2.9 broadcast_multiply_fusion
  (151 shorter events, 56.8 us)
Async XLA Ops:
  82.4 27.8 %copy-start = (bf16[64,32,128]{2,1,0:T(8,128)(2,1)S(1)}, bf16[64,32,128]{2,1,0:T(8,128)(2,1)}, u32[]{:S(2)}) copy-start(bf16[64,32,128]{2,1,0:T(8,128)(2,1)} %param.4) | copy-start | bytes 1572868
  110.7 4.1 collective-permute-start
  113.5 9.9 %collective-permute-start.1 = (bf16[2,32,128]{2,1,0:T(8,128)(2,1)S(1)}, bf16[2,32,128]{2,1,0:T(8,128)(2,1)S(1)}, u32[]{:S(2)}, u32[]{:S(2)}) collective-permute-start(bf16[2,32,128]{2,1,0:T(8,128)(2,1)S(1)} %get-tuple-element.34), channel_id=1, source_target_pairs={{32,0},{64,32},{96,64},{128,96},{160,128},{192,160},{224,192},{256... | collective-permute-start | bytes 49160 | tf_op jit(solution)/shard_map/ppermute | solution.py:17
  123.5 5.3 collective-permute-start.2
  126.8 5.3 collective-permute-start.3
  132.6 1.2 copy-start.17
  132.6 1.2 copy-start.21
  137.7 109.9 %copy-start.15 = (bf16[64,32,128]{2,1,0:T(8,128)(2,1)}, bf16[64,32,128]{2,1,0:T(8,128)(2,1)S(1)}, u32[]{:S(2)}) copy-start(bf16[64,32,128]{2,1,0:T(8,128)(2,1)S(1)} %get-tuple-element.38) | copy-start | bytes 1572868
  137.7 4.9 collective-permute-start.4
  141.3 8.8 %collective-permute-start.5 = (bf16[4,32,128]{2,1,0:T(8,128)(2,1)S(1)}, bf16[4,32,128]{2,1,0:T(8,128)(2,1)S(1)}, u32[]{:S(2)}, u32[]{:S(2)}) collective-permute-start(bf16[4,32,128]{2,1,0:T(8,128)(2,1)S(1)} %get-tuple-element.32), channel_id=1, source_target_pairs={{32,0},{64,32},{96,64},{128,96},{160,128},{192,160},{224,192},{256... | collective-permute-start | bytes 98312 | tf_op jit(solution)/shard_map/ppermute | solution.py:17
  150.2 5.6 collective-permute-start.6
  153.3 5.7 collective-permute-start.7
  163.9 54.3 %copy-start.19 = (f32[1,64,32,128]{3,0,2,1:T(1,128)}, f32[1,64,32,128]{3,0,2,1:T(1,128)S(1)}, u32[]{:S(2)}) copy-start(f32[1,64,32,128]{3,0,2,1:T(1,128)S(1)} %fusion.11) | copy-start | bytes 3145732
  164.7 7.1 collective-permute-start.8
  170.5 5.3 collective-permute-start.9
  175.8 8.4 collective-permute-start.10
  178.8 6.6 collective-permute-start.11
  182.8 65.6 %copy-start.3 = (f32[64,1,32,128]{3,0,2,1:T(8,128)}, f32[64,1,32,128]{3,0,2,1:T(8,128)S(1)}, u32[]{:S(2)}) copy-start(f32[64,1,32,128]{3,0,2,1:T(8,128)S(1)} %slice.262) | copy-start | bytes 3145732
  184.1 70.8 %copy-start.6 = (bf16[72,36,128]{2,1,0:T(8,128)(2,1)}, bf16[72,36,128]{2,1,0:T(8,128)(2,1)S(1)}, u32[]{:S(2)}) copy-start(bf16[72,36,128]{2,1,0:T(8,128)(2,1)S(1)} %get-tuple-element.12) | copy-start | bytes 1990660
  185.5 4.9 copy-start.14
  191.8 7.5 collective-permute-start.12
  195.6 5.3 collective-permute-start.13
  200.9 6.0 collective-permute-start.14
  204.4 8.0 collective-permute-start.15
  219.1 5.7 collective-permute-start.16
  223.1 4.7 collective-permute-start.17
  227.8 5.7 collective-permute-start.18
  231.0 11.7 %collective-permute-start.19 = (bf16[72,4,128]{2,1,0:T(4,128)(2,1)S(1)}, bf16[72,4,128]{2,1,0:T(4,128)(2,1)S(1)}, u32[]{:S(2)}, u32[]{:S(2)}) collective-permute-start(bf16[72,4,128]{2,1,0:T(4,128)(2,1)S(1)} %get-tuple-element.14), channel_id=1, source_target_pairs={{1,0},{2,1},{3,2},{4,3},{5,4},{6,5},{7,6},{8,7},{9,8},{10,9},{11,1... | collective-permute-start | bytes 221192 | tf_op jit(solution)/shard_map/ppermute | solution.py:17
  233.5 14.1 %copy-start.12 = (f32[9,128,128]{2,1,0:T(8,128)}, f32[9,128,128]{2,1,0:T(8,128)S(1)}, u32[]{:S(2)}) copy-start(f32[9,128,128]{2,1,0:T(8,128)S(1)} %fusion.44) | copy-start | bytes 1769476
  248.4 27.9 %copy-start.1 = (bf16[64,32,128]{2,1,0:T(8,128)(2,1)}, bf16[64,32,128]{2,1,0:T(8,128)(2,1)S(1)}, u32[]{:S(2)}) copy-start(bf16[64,32,128]{2,1,0:T(8,128)(2,1)S(1)} %fusion.87) | copy-start | bytes 1572868
  249.7 6.3 collective-permute-start.20
  253.7 4.5 collective-permute-start.21
  258.2 6.7 collective-permute-start.22
  261.5 12.0 %collective-permute-start.23 = (bf16[68,2,128]{2,1,0:T(2,128)(2,1)S(1)}, bf16[68,2,128]{2,1,0:T(2,128)(2,1)S(1)}, u32[]{:S(2)}, u32[]{:S(2)}) collective-permute-start(bf16[68,2,128]{2,1,0:T(2,128)(2,1)S(1)} %get-tuple-element.20), channel_id=1, source_target_pairs={{1,0},{2,1},{3,2},{4,3},{5,4},{6,5},{7,6},{8,7},{9,8},{10,9},{11,1... | collective-permute-start | bytes 104456 | tf_op jit(solution)/shard_map/ppermute | solution.py:17
  278.6 61.7 %all-to-all-start.3 = ((bf16[64,32,128]{2,1,0:T(8,128)(2,1)}), bf16[64,32,128]{2,1,0:T(8,128)(2,1)}, u32[]{:S(2)}, u32[]{:S(2)}) async-start(bf16[64,32,128]{2,1,0:T(8,128)(2,1)} %bitcast.326), calls=%async_computation.3 | async-start | bytes 1048576 | tf_op jit(solution)/shard_map/all_to_all | solution.py:47
  312.5 2.2 copy-start.7
  314.6 1.0 copy-start.16
  315.7 1.2 copy-start.5
  319.8 1.2 copy-start.20
  321.0 1.1 copy-start.9
  342.7 6.6 copy-start.8
  342.7 19.3 %all-to-all-start.4 = ((bf16[2,1024,128]{2,0,1:T(2,128)(2,1)}), bf16[2,1024,128]{2,0,1:T(2,128)(2,1)S(1)}, u32[]{:S(2)}, u32[]{:S(2)}) async-start(bf16[2,1024,128]{2,0,1:T(2,128)(2,1)} %copy.263), calls=%async_computation.4 | async-start | bytes 1048576 | tf_op jit(solution)/shard_map/all_to_all | solution.py:49
  349.2 1.1 copy-start.10
  354.2 1.4 copy-start.4
  362.9 496.3 %all-to-all-start.5 = ((bf16[32,64,128]{2,1,0:T(8,128)(2,1)}), bf16[32,64,128]{2,1,0:T(8,128)(2,1)S(1)}, u32[]{:S(2)}, u32[]{:S(2)}) async-start(bf16[32,64,128]{2,1,0:T(8,128)(2,1)} %bitcast.53), calls=%async_computation.5 | async-start | bytes 1048576 | tf_op jit(solution)/shard_map/all_to_all | solution.py:48
  372.8 1.7 copy-start.11
  372.8 481.8 %all-reduce.3.cloned.1.call-start = ((), (), s32[]{:S(2)}) async-start(), calls=%async_computation.6 | async-start | bytes 3932160 | tf_op jit(solution)/shard_map/psum | solution.py:130
  372.9 1.7 copy-start.13
  (2 other events, 1.9 us)
Sparse Core Ops, SparseCore 0:
  379.5 475.1 all-reduce.2
where the time goes:
time: 875 us; the launch traced here: 867 us
  waiting for transfers between devices  558 us (64%)
  starting transfers between devices  114 us (13%)
  blocking collectives  101 us (12%)
  matrix products  51.5 us (6%)
  other arithmetic  17.3 us (2%)
  between operations  15.1 us (2%)
  local copies, waits for them, and re-layouts  10.8 us (1%)
    psum x1, waiting for transfers between devices, body(): conv_stack, proj_stack = lax.psum((conv_stack, proj_stack), ('row', 'col'))  478 us
    ppermute x12, waiting for transfers between devices, with_halo(): lax.ppermute(head, axis, [((i + 1) % count, i) for i in range(ends)])  57.8 us
    all_to_all x1, blocking collectives, mirror(): lax.all_to_all(sectioned, 'col', split_axis=0, concat_axis=1, tiled=True)  48.3 us
    ppermute x12, starting transfers between devices, with_halo(): lax.ppermute(tail, axis, [(i, (i + 1) % count) for i in range(ends)])  43.2 us
    all_to_all x1, starting transfers between devices, mirror(): lax.all_to_all(sectioned, 'col', split_axis=0, concat_axis=1, tiled=True)  33.9 us
    all_to_all x1, blocking collectives, mirror(): lax.all_to_all(lax.all_to_all(sectioned, 'row', split_axis=1, concat_axis...  27.6 us
    all_to_all x1, blocking collectives, mirror(): lax.all_to_all(sectioned, 'row', split_axis=1, concat_axis=0, tiled=True)  25.2 us
    conv_general_dilated x6, matrix products, dilated_valid(): lax.conv_general_dilated(widened[None], kernel, (1, 1), 'VALID', rhs_dila...  22.7 us
  transfers between devices with their start and end apart: 28, of which 15 were waited for; matrix products, arithmetic and copies ran while one was open for 4% of the time, Pallas kernels for 0%

commit v1 on v0

v1 whole, which is shorter than its diff:
```python
import functools

import jax
import jax.numpy as jnp
from jax import lax
from jax.experimental import pallas as pl
from jax.experimental.pallas import tpu as pltpu
from jax.sharding import PartitionSpec as P

MESH = pl.DeviceIdType.MESH
BF = jnp.bfloat16
F32 = jnp.float32
ROWS, COLS, CH, MARGIN = 64, 32, 128, 8
CELLS = ROWS * COLS
HIGH, WIDE = ROWS + 2 * MARGIN, COLS + 2 * MARGIN
STEP = 8
CHUNK = STEP * COLS
CHUNKS = ROWS // STEP
TAPS = 9
BLOCKS = 3
SLOPE_C = 0.7978845608028654
CUBIC = 0.044715
MOVES = ((0, -1), (0, 1), (-1, 0), (1, 0), (-1, -1), (-1, 1), (1, -1), (1, 1))
GROUPS = ((2, 1), (0,))
BLOCK_ROWS = (TAPS + 1) * CH


def gelu_parts(v):
    u = v * v
    t = jnp.tanh(SLOPE_C * v * (1.0 + CUBIC * u))
    half = 0.5 + 0.5 * t
    slope = half + (0.5 * SLOPE_C) * v * (1.0 - t * t) * (1.0 + 3.0 * CUBIC * u)
    return v * half, slope


def dot(a, b):
    return jnp.dot(a, b, preferred_element_type=F32)


def dot_nt(a, b):
    return lax.dot_general(a, b, (((1,), (1,)), ((), ())), preferred_element_type=F32)


def dot_tn(a, b):
    return lax.dot_general(a, b, (((0,), (0,)), ((), ())), preferred_element_type=F32)


class Place:
    def __init__(self, rows, cols):
        self.rows, self.cols = rows, cols
        self.side = 4 if rows >= 16 else 2
        self.depth = (rows // self.side) * (cols // (2 * self.side))
        self.parts = rows // self.side
        self.r, self.c = lax.axis_index("row"), lax.axis_index("col")
        self.y, self.zl = self.r % self.side, self.r // self.side
        self.k = self.c % 2
        self.q = self.c // 2
        self.x, self.zh = self.q % self.side, self.q // self.side
        self.z = self.zh * self.parts + self.zl

    def at_core(self):
        return (self.r, self.c + 1 - 2 * self.k)

    def at_x(self, offset):
        x = (self.x + offset) % self.side
        return (self.r, self.zh * 2 * self.side + 2 * x + self.k)

    def at_y(self, offset):
        y = (self.y + offset) % self.side
        return (self.zl * self.side + y, self.c)

    def at_z(self, z):
        zh, zl = z // self.parts, z % self.parts
        return (zl * self.side + self.y, zh * 2 * self.side + 2 * self.x + self.k)

    def inside(self, dr, dc):
        r, c = self.r + dr, self.c + dc
        return (r >= 0) & (r < self.rows) & (c >= 0) & (c < self.cols)


class Sent:
    def __init__(self):
        self.items = []

    def start(self, cond, copy):
        if cond is None:
            copy.start()
        else:
            pl.when(cond)(copy.start)
        self.items.append((cond, copy))

    def finish(self):
        for cond, copy in self.items:
            if cond is None:
                copy.wait_send()
            else:
                pl.when(cond)(copy.wait_send)


def remote(src, dst, send, recv, device):
    return pltpu.make_async_remote_copy(
        src_ref=src, dst_ref=dst, send_sem=send, recv_sem=recv, device_id=device, device_id_type=MESH
    )


class Reduce:
    @staticmethod
    def sizes(n, side, depth):
        half = n // 2
        xq = half // side
        yq = xq // side
        tiles = yq // 8
        zr = 8 * -(-tiles // depth)
        return half, xq, yq, zr

    @staticmethod
    def scratch(n, side, depth):
        half, xq, yq, zr = Reduce.sizes(n, side, depth)
        dma = pltpu.SemaphoreType.DMA
        return [
            pltpu.VMEM((n, CH), BF),
            pltpu.VMEM((half, CH), BF),
            pltpu.VMEM((half, CH), BF),
            pltpu.VMEM((side - 1, xq, CH), BF),
            pltpu.VMEM((xq, CH), F32),
            pltpu.VMEM((side - 1, yq, CH), F32),
            pltpu.VMEM((yq, CH), F32),
            pltpu.VMEM((depth, zr, CH), F32),
            pltpu.VMEM((yq, CH), F32),
            pltpu.VMEM((xq, CH), F32),
            pltpu.VMEM((xq, CH), BF),
            pltpu.VMEM((half, CH), BF),
            pltpu.VMEM((n, CH), BF),
            dma((4, 4)),
            dma((4, 4)),
            dma((4,)),
            dma((4,)),
            dma((2, depth)),
            dma((2, depth)),
        ]

    def __init__(self, n, place, sent, refs):
        self.n, self.p, self.sent = n, place, sent
        self.half, self.xq, self.yq, self.zr = Reduce.sizes(n, place.side, place.depth)
        self.owners = self.yq // self.zr
        (self.src, self.rc, self.s1, self.rx, self.s2, self.ry, self.s3, self.rz, self.g3, self.g2,
         self.g2b, self.g1, self.fin, self.ssem, self.rsem, self.csend, self.crecv, self.zsend,
         self.zrecv) = refs
        self.waits = []

    def rows(self, index, size):
        return pl.ds(pl.multiple_of(index * size, 8), size)

    def rows16(self, index, size):
        return pl.ds(pl.multiple_of(index * size, 16), size)

    def _wait(self):
        for copy in self.waits:
            copy.wait_recv()
        self.waits = []

    def _send(self, src, dst, send, recv, device):
        copy = remote(src, dst, send, recv, device)
        self.sent.start(None, copy)
        self.waits.append(copy)

    def core_start(self):
        p = self.p
        self._send(self.src.at[self.rows16(1 - p.k, self.half)], self.rc, self.csend.at[0], self.crecv.at[0], p.at_core())

    def core_add(self):
        self._wait()
        own = self.rows16(self.p.k, self.half)
        self.s1[...] = (self.src[own, :].astype(F32) + self.rc[...].astype(F32)).astype(BF)

    def x_start(self):
        p = self.p
        for o in range(1, p.side):
            other = (p.x + o) % p.side
            self._send(self.s1.at[self.rows16(other, self.xq)], self.rx.at[o - 1], self.ssem.at[0, o], self.rsem.at[0, o], p.at_x(o))

    def x_add(self):
        self._wait()
        total = self.s1[self.rows16(self.p.x, self.xq), :].astype(F32)
        for o in range(1, self.p.side):
            total = total + self.rx[o - 1].astype(F32)
        self.s2[...] = total

    def y_start(self):
        p = self.p
        for o in range(1, p.side):
            other = (p.y + o) % p.side
            self._send(self.s2.at[self.rows(other, self.yq)], self.ry.at[o - 1], self.ssem.at[1, o], self.rsem.at[1, o], p.at_y(o))

    def y_add(self):
        self._wait()
        total = self.s2[self.rows(self.p.y, self.yq), :]
        for o in range(1, self.p.side):
            total = total + self.ry[o - 1]
        self.s3[...] = total

    def _z_out(self, o):
        p = self.p
        z = (p.z + o) % p.depth
        return z, remote(self.s3.at[self.rows(z, self.zr)], self.rz.at[o], self.zsend.at[0, o], self.zrecv.at[0, o], p.at_z(z))

    def z_start(self):
        def body(o, _):
            z = (self.p.z + o) % self.p.depth

            @pl.when(z < self.owners)
            def _():
                self._z_out(o)[1].start()

            return 0

        lax.fori_loop(1, self.p.depth, body, 0)

    def z_add(self):
        p = self.p

        @pl.when(p.z < self.owners)
        def _():
            def wait(o, _):
                remote(self.rz.at[o], self.rz.at[o], self.zsend.at[0, o], self.zrecv.at[0, o], p.at_z(p.z)).wait_recv()
                return 0

            lax.fori_loop(1, p.depth, wait, 0)
            own = self.rows(p.z, self.zr)
            total = self.s3[own, :]
            for o in range(1, p.depth):
                total = total + self.rz[o]
            self.g3[own, :] = total

    def _z_back(self, o):
        p = self.p
        z = (p.z + o) % p.depth
        own = self.g3.at[self.rows(p.z, self.zr)]
        return remote(own, own, self.zsend.at[1, o], self.zrecv.at[1, p.z], p.at_z(z))

    def zg_start(self):
        p = self.p

        @pl.when(p.z < self.owners)
        def _():
            def body(o, _):
                self._z_back(o).start()
                return 0

            lax.fori_loop(1, p.depth, body, 0)

    def zg_wait(self):
        p = self.p

        def body(z, _):
            @pl.when(z != p.z)
            def _():
                part = self.g3.at[self.rows(z, self.zr)]
                remote(part, part, self.zsend.at[1, z], self.zrecv.at[1, z], p.at_z(z)).wait_recv()

            return 0

        lax.fori_loop(0, self.owners, body, 0)

    def yg_start(self):
        p = self.p
        own = self.rows(p.y, self.yq)
        for o in range(1, p.side):
            copy = remote(self.g3, self.g2.at[own], self.ssem.at[2, o], self.rsem.at[2, o], p.at_y(o))
            self.sent.start(None, copy)
            other = self.rows((p.y + p.side - o) % p.side, self.yq)
            self.waits.append(remote(self.g3, self.g2.at[other], self.ssem.at[2, o], self.rsem.at[2, o], p.at_y(o)))
        self.g2[own, :] = self.g3[...]

    def xg_start(self):
        self._wait()
        p = self.p
        self.g2b[...] = self.g2[...].astype(BF)
        own = self.rows16(p.x, self.xq)
        for o in range(1, p.side):
            copy = remote(self.g2b, self.g1.at[own], self.ssem.at[3, o], self.rsem.at[3, o], p.at_x(o))
            self.sent.start(None, copy)
            other = self.rows16((p.x + p.side - o) % p.side, self.xq)
            self.waits.append(remote(self.g2b, self.g1.at[other], self.ssem.at[3, o], self.rsem.at[3, o], p.at_x(o)))
        self.g1[own, :] = self.g2b[...]

    def cg_start(self):
        self._wait()
        p = self.p
        own = self.rows16(p.k, self.half)
        other = self.rows16(1 - p.k, self.half)
        self.sent.start(None, remote(self.g1, self.fin.at[own], self.csend.at[1], self.crecv.at[1], p.at_core()))
        self.waits.append(remote(self.g1, self.fin.at[other], self.csend.at[1], self.crecv.at[1], p.at_core()))
        self.fin[own, :] = self.g1[...]

    def done(self):
        self._wait()

    def finish_sends(self):
        def body(o, _):
            z = (self.p.z + o) % self.p.depth

            @pl.when(z < self.owners)
            def _():
                self._z_out(o)[1].wait_send()

            @pl.when(self.p.z < self.owners)
            def _():
                self._z_back(o).wait_send()

            return 0

        lax.fori_loop(1, self.p.depth, body, 0)


def kernel(rows, cols, *refs):
    (contact, cotangent, conv_w, proj_w, out_map, out_conv, out_proj,
     own, grad, wf, wb, pw, hid, hslope, mid, slope, sh, wide, left, right, pack, mir, flat, acc, accp,
     hsend, hrecv, msend, mrecv, mloc, loc) = refs[:31]
    p = Place(rows, cols)
    sent = Sent()
    per = (len(refs) - 31) // len(GROUPS)
    reduces = []
    for index, blocks in enumerate(GROUPS):
        start = 31 + index * per
        reduces.append(Reduce(len(blocks) * BLOCK_ROWS, p, sent, refs[start : start + per]))

    barrier = pltpu.get_barrier_semaphore()

    def greet(device):
        pl.semaphore_signal(barrier, inc=1, device_id=device, device_id_type=MESH)

    count = jnp.int32(1 + 2 * (p.side - 1) + p.depth - 1)
    greet(p.at_core())
    for o in range(1, p.side):
        greet(p.at_x(o))
        greet(p.at_y(o))

    def greet_z(o, _):
        greet(p.at_z((p.z + o) % p.depth))
        return 0

    lax.fori_loop(1, p.depth, greet_z, 0)
    for dr, dc in MOVES:
        there = p.inside(dr, dc)
        pl.when(there)(functools.partial(greet, (p.r + dr, p.c + dc)))
        count = count + there.astype(jnp.int32)
    apart = p.q != p.r
    for h in range(2):
        pl.when(apart)(functools.partial(greet, (p.q, 2 * p.r + h)))
        count = count + apart.astype(jnp.int32)

    loads = [
        pltpu.make_async_copy(contact, own, loc.at[0]),
        pltpu.make_async_copy(cotangent, grad, loc.at[1]),
        pltpu.make_async_copy(conv_w, wf, loc.at[2]),
        pltpu.make_async_copy(proj_w, pw, loc.at[3]),
    ]
    for load in loads:
        load.start()
    pl.semaphore_wait(barrier, count)

    half = CELLS // 2

    def mirror_copies(turn, source, h):
        stays = (p.q == p.r) & (p.k == h)
        src = source.at[pl.ds(h * half, half)]
        dst = mir.at[turn, p.k]
        there = remote(src, dst, msend.at[turn, h], mrecv.at[turn, p.k], (p.q, 2 * p.r + h))
        here = pltpu.make_async_copy(src, dst, mloc.at[turn])
        return stays, there, here

    def mirror_start(turn, source, h):
        stays, there, here = mirror_copies(turn, source, h)
        sent.start(jnp.logical_not(stays), there)
        pl.when(stays)(here.start)

    def mirror_wait(turn, source):
        for h in range(2):
            stays = (p.q == p.r) & (p.k == h)
            dst = mir.at[turn, h]
            src = source.at[pl.ds(0, half)]
            there = remote(src, dst, msend.at[turn, h], mrecv.at[turn, h], (p.q, 2 * p.r + h))
            here = pltpu.make_async_copy(src, dst, mloc.at[turn])
            pl.when(jnp.logical_not(stays))(there.wait_recv)
            pl.when(stays)(here.wait)

    def mirror_spread(turn):
        def body(i, _):
            flat[pl.ds(pl.multiple_of(i * CHUNK, CHUNK), CHUNK), :] = mir[
                turn, i // 4, pl.ds(pl.multiple_of((i % 4) * CHUNK, CHUNK), CHUNK), :
            ].astype(F32)
            return 0

        lax.fori_loop(0, CELLS // CHUNK, body, 0)

    def mirror_rows(chunk):
        base = (chunk // (COLS // STEP)) * half + (chunk % (COLS // STEP)) * STEP
        return jnp.concatenate([flat[pl.ds(base + j, COLS, stride=COLS), :] for j in range(STEP)], axis=0)

    for h in range(2):
        mirror_start(0, contact, h)

    zero = functools.partial(jnp.zeros, dtype=BF)
    corner = MARGIN * MARGIN
    low, side_rows = (MARGIN + ROWS) * MARGIN, ROWS * MARGIN

    def fill(dr, dc, ref, start, size):
        @pl.when(jnp.logical_not(p.inside(dr, dc)))
        def _():
            def body(e, _):
                if ref is sh:
                    sh[e, 1, pl.ds(start, size), :] = zero((size, CH))
                else:
                    ref[e, pl.ds(start, size), :] = zero((size, CH))
                return 0

            lax.fori_loop(0, 2 * BLOCKS, body, 0)

    fill(-1, 0, sh, 0, MARGIN * COLS)
    fill(1, 0, sh, (MARGIN + ROWS) * COLS, MARGIN * COLS)
    for dc, ref in ((-1, left), (1, right)):
        fill(-1, dc, ref, 0, corner)
        fill(0, dc, ref, corner, side_rows)
        fill(1, dc, ref, low, corner)

    loads[2].wait()
    loads[3].wait()

    def flip(index, _):
        block, tap = index // TAPS, index % TAPS
        tile = wf[block, pl.ds(pl.multiple_of(tap * CH, CH), CH), :].astype(F32)
        wb[block, pl.ds(pl.multiple_of((TAPS - 1 - tap) * CH, CH), CH), :] = tile.T.astype(BF)
        return 0

    lax.fori_loop(0, BLOCKS * TAPS, flip, 0)
    loads[0].wait()
    loads[1].wait()

    def cells(chunk):
        return pl.ds(pl.multiple_of(chunk * CHUNK, CHUNK), CHUNK)

    def put_center(e, chunk, values):
        rounded = values.astype(BF)
        sh[e, 1, pl.ds(pl.multiple_of(chunk * CHUNK + MARGIN * COLS, CHUNK), CHUNK), :] = rounded
        cube = values.reshape(STEP, COLS, CH)
        wide[pl.ds(chunk * STEP + MARGIN, STEP), MARGIN : MARGIN + COLS, :] = cube
        edge = STEP * MARGIN
        at = pl.ds(pl.multiple_of(chunk * edge, edge), edge)
        pack[e, 0, at, :] = cube[:, :MARGIN, :].reshape(edge, CH).astype(BF)
        pack[e, 1, at, :] = cube[:, COLS - MARGIN :, :].reshape(edge, CH).astype(BF)

    def halo_copy(e, d, index):
        dr, dc = MOVES[index]
        strip = d * COLS
        if dr == 0:
            src, dst = pack.at[e, (dc + 1) // 2], (right if dc < 0 else left).at[e, pl.ds(corner, side_rows)]
        elif dc == 0:
            start, end = (MARGIN, MARGIN + ROWS) if dr < 0 else (MARGIN + ROWS - d, MARGIN - d)
            src = sh.at[e, 1, pl.ds(start * COLS, strip)]
            dst = sh.at[e, 1, pl.ds(end * COLS, strip)]
        else:
            src = pack.at[e, (dc + 1) // 2, pl.ds(0 if dr < 0 else side_rows - corner, corner)]
            dst = (right if dc < 0 else left).at[e, pl.ds(low if dr < 0 else 0, corner)]
        return remote(src, dst, hsend.at[e, index], hrecv.at[e, index], (p.r + dr, p.c + dc))

    def halo_start(e, d):
        for index, (dr, dc) in enumerate(MOVES):
            sent.start(p.inside(dr, dc), halo_copy(e, d, index))

    def halo_wait(e, d):
        for index, (dr, dc) in enumerate(MOVES):
            pl.when(p.inside(-dr, -dc))(halo_copy(e, d, index).wait_recv)

    def halo_build(e, d):
        def sides(i, _):
            at = pl.ds(pl.multiple_of(i * corner, corner), corner)
            to = pl.ds(i * MARGIN, MARGIN)
            wide[to, :MARGIN, :] = left[e, at, :].astype(F32).reshape(MARGIN, MARGIN, CH)
            wide[to, MARGIN + COLS :, :] = right[e, at, :].astype(F32).reshape(MARGIN, MARGIN, CH)
            return 0

        lax.fori_loop(0, HIGH // MARGIN, sides, 0)
        for start in (MARGIN - d, MARGIN + ROWS):
            strip = sh[e, 1, start * COLS : (start + d) * COLS, :].astype(F32)
            wide[start : start + d, MARGIN : MARGIN + COLS, :] = strip.reshape(d, COLS, CH)

        def shift(i, _):
            first = MARGIN - d + 4 * i
            for b in (0, 2):
                begin = MARGIN + (b - 1) * d
                cube = wide[pl.ds(first, 4), begin : begin + COLS, :]
                sh[e, b, pl.ds(pl.multiple_of(first * COLS, 2 * COLS), 4 * COLS), :] = cube.reshape(4 * COLS, CH).astype(BF)
            return 0

        lax.fori_loop(0, (ROWS + 2 * d) // 4, shift, 0)

    def windows(e, d, chunk):
        taps = []
        for a in range(3):
            start = pl.multiple_of(chunk * CHUNK + (MARGIN + (a - 1) * d) * COLS, 2 * COLS)
            for b in range(3):
                taps.append(sh[e, b, pl.ds(start, CHUNK), :])
        return jnp.concatenate(taps, axis=1)

    def each_chunk(body):
        def run(chunk, _):
            body(chunk)
            return 0

        lax.fori_loop(0, CHUNKS, run, 0)

    mirror_wait(0, contact)
    mirror_spread(0)

    def first(chunk):
        at = cells(chunk)
        hidden = (0.5 * (own[at, :].astype(F32) + mirror_rows(chunk))).astype(BF)
        hid[0, at, :] = hidden
        act, steep = gelu_parts(hidden.astype(F32))
        hslope[0, at, :] = steep
        put_center(0, chunk, act)

    each_chunk(first)

    for k in range(BLOCKS):
        d = 2 ** (k + 1)
        halo_start(k, d)
        halo_wait(k, d)
        halo_build(k, d)

        def forward(chunk, k=k, d=d):
            at = cells(chunk)
            middle, steep = gelu_parts(dot(windows(k, d, chunk), wf[k]))
            middle = middle.astype(BF)
            mid[k, at, :] = middle
            slope[k, at, :] = steep
            if k + 1 < BLOCKS:
                hidden = (hid[k, at, :].astype(F32) + dot(middle, pw[k])).astype(BF)
                hid[k + 1, at, :] = hidden
                act, bend = gelu_parts(hidden.astype(F32))
                hslope[k + 1, at, :] = bend
                put_center(k + 1, chunk, act)
            else:
                put_center(k + 1, chunk, dot_nt(grad[at, :], pw[k]) * steep)

        each_chunk(forward)

    queue = []

    def advance(steps):
        for _ in range(steps):
            if queue:
                queue.pop(0)()

    def phases(red):
        def both(a, b):
            def run():
                a()
                b()

            return run

        return [
            red.core_start,
            both(red.core_add, red.x_start),
            both(red.x_add, red.y_start),
            both(red.y_add, red.z_start),
            both(red.z_add, red.zg_start),
            both(red.zg_wait, red.yg_start),
            red.xg_start,
            red.cg_start,
            red.done,
        ]

    for k in reversed(range(BLOCKS)):
        d = 2 ** (k + 1)
        e = 2 * BLOCKS - 1 - k
        halo_start(e, d)
        advance(1)
        acc[...] = jnp.zeros_like(acc)
        accp[...] = jnp.zeros_like(accp)

        def weights(chunk, k=k, d=d, e=e):
            at = cells(chunk)
            back = sh[e, 1, pl.ds(pl.multiple_of(chunk * CHUNK + MARGIN * COLS, CHUNK), CHUNK), :]
            acc[...] += dot_tn(back, windows(k, d, chunk))
            accp[...] += dot_tn(mid[k, at, :], grad[at, :])

        each_chunk(weights)
        group = next(i for i, blocks in enumerate(GROUPS) if k in blocks)
        base = GROUPS[group].index(k) * BLOCK_ROWS
        red = reduces[group]
        for tap in range(TAPS):
            red.src[base + tap * CH : base + (tap + 1) * CH, :] = acc[:, tap * CH : (tap + 1) * CH].T.astype(BF)
        red.src[base + TAPS * CH : base + BLOCK_ROWS, :] = accp[...].astype(BF)
        if k == GROUPS[group][-1]:
            queue.extend(phases(red))
        advance(1)
        halo_wait(e, d)
        halo_build(e, d)
        advance(1)

        def backward(chunk, k=k, d=d, e=e):
            at = cells(chunk)
            change = dot(windows(e, d, chunk), wb[k]) * hslope[k, at, :]
            new = (grad[at, :].astype(F32) + change).astype(BF)
            grad[at, :] = new
            if k > 0:
                put_center(e + 1, chunk, dot_nt(new, pw[k - 1]) * slope[k - 1, at, :])

        each_chunk(backward)

    for h in range(2):
        mirror_start(1, grad, h)
    while queue:
        advance(1)
    scale = 1.0 / (rows * ROWS)
    for group, blocks in enumerate(GROUPS):
        for place, k in enumerate(blocks):
            base = place * BLOCK_ROWS
            fin = reduces[group].fin
            out_conv[k, :, :] = fin[base : base + TAPS * CH, :].astype(F32) * scale
            out_proj[k, :, :] = fin[base + TAPS * CH : base + BLOCK_ROWS, :].astype(F32) * scale
    mirror_wait(1, grad)
    mirror_spread(1)

    def last(chunk):
        at = cells(chunk)
        out_map[at, :] = (0.5 * (grad[at, :].astype(F32) + mirror_rows(chunk))).astype(BF)

    each_chunk(last)
    sent.finish()
    for red in reduces:
        red.finish_sends()


def solution(mesh):
    rows, cols = mesh.shape["row"], mesh.shape["col"]
    side = 4 if rows >= 16 else 2
    depth = (rows // side) * (cols // (2 * side))
    vmem, dma = pltpu.VMEM, pltpu.SemaphoreType.DMA
    scratch = [
        vmem((CELLS, CH), BF),
        vmem((CELLS, CH), BF),
        vmem((BLOCKS, TAPS * CH, CH), BF),
        vmem((BLOCKS, TAPS * CH, CH), BF),
        vmem((BLOCKS, CH, CH), BF),
        vmem((BLOCKS, CELLS, CH), BF),
        vmem((BLOCKS, CELLS, CH), F32),
        vmem((BLOCKS, CELLS, CH), BF),
        vmem((BLOCKS, CELLS, CH), F32),
        vmem((2 * BLOCKS, 3, HIGH * COLS, CH), BF),
        vmem((HIGH, WIDE, CH), F32),
        vmem((2 * BLOCKS, HIGH * MARGIN, CH), BF),
        vmem((2 * BLOCKS, HIGH * MARGIN, CH), BF),
        vmem((2 * BLOCKS, 2, ROWS * MARGIN, CH), BF),
        vmem((2, 2, CELLS // 2, CH), BF),
        vmem((CELLS, CH), F32),
        vmem((CH, TAPS * CH), F32),
        vmem((CH, CH), F32),
        dma((2 * BLOCKS, 8)),
        dma((2 * BLOCKS, 8)),
        dma((2, 2)),
        dma((2, 2)),
        dma((2,)),
        dma((4,)),
    ]
    for blocks in GROUPS:
        scratch += Reduce.scratch(len(blocks) * BLOCK_ROWS, side, depth)

    def body(contact_map, cotangent, conv_weight, proj_weight):
        out_map, out_conv, out_proj = pl.pallas_call(
            functools.partial(kernel, rows, cols),
            out_shape=(
                jax.ShapeDtypeStruct((CELLS, CH), BF),
                jax.ShapeDtypeStruct((BLOCKS, TAPS * CH, CH), F32),
                jax.ShapeDtypeStruct((BLOCKS, CH, CH), F32),
            ),
            in_specs=[pl.BlockSpec(memory_space=pl.ANY)] * 4,
            out_specs=(pl.BlockSpec(memory_space=pltpu.VMEM),) * 3,
            scratch_shapes=scratch,
            compiler_params=pltpu.CompilerParams(
                collective_id=0, has_side_effects=True, vmem_limit_bytes=56 * 1024 * 1024
            ),
        )(
            contact_map.reshape(CELLS, CH),
            cotangent.reshape(CELLS, CH),
            conv_weight.reshape(BLOCKS, TAPS * CH, CH),
            proj_weight,
        )
        return (
            out_map.reshape(ROWS, COLS, CH),
            out_conv.reshape(BLOCKS, 3, 3, CH, CH),
            out_proj,
        )

    in_specs = (P("row", "col", None), P("row", "col", None), P(), P())
    out_specs = (P("row", "col", None), P(), P())
    return jax.shard_map(body, mesh=mesh, in_specs=in_specs, out_specs=out_specs, check_vma=False)
```

time: 875 us -> 255 us (0.29)
  waiting for transfers between devices: 558 us -> 0 us
  Pallas kernels: 0 us -> 249 us
  starting transfers between devices: 114 us -> 0 us
  blocking collectives: 101 us -> 0 us
  matrix products: 51.5 us -> 0 us
  other arithmetic: 17.3 us -> 0 us
  between operations: 15.1 us -> 0.64 us
    psum x1 -> x0, waiting for transfers between devices: 478 us -> none  [body(): conv_stack, proj_stack = lax.psum((conv_stack, proj_stack), ('row', 'col'))]
    pallas_call x0 -> x1, Pallas kernels: none -> 249 us  [body(): pl.pallas_call(functools.partial(kernel, rows, cols), out_shape=(jax.Shap...]
    all_to_all x3 -> x0, blocking collectives: 101 us -> none  [the longest x1 48.3 us: mirror(): lax.all_to_all(sectioned, 'col', split_axis=0, concat_axis=1, tiled=True)]
    ppermute x24 -> x0, starting transfers between devices: 64.1 us -> none  [the longest x12 43.2 us: with_halo(): lax.ppermute(tail, axis, [(i, (i + 1) % count) for i in range(ends)])]
    ppermute x24 -> x0, waiting for transfers between devices: 57.9 us -> none  [the longest x12 57.8 us: with_halo(): lax.ppermute(head, axis, [((i + 1) % count, i) for i in range(ends)])]
    all_to_all x3 -> x0, starting transfers between devices: 49.4 us -> none  [the longest x1 33.9 us: mirror(): lax.all_to_all(sectioned, 'col', split_axis=0, concat_axis=1, tiled=True)]
    dot_general x35 -> x0, matrix products: 28.7 us -> none  [the longest x27 22.1 us: body(): lax.dot_general(window.reshape(-1, channels), flat_back, contract_rows, p...]
    conv_general_dilated x6 -> x0, matrix products: 22.7 us -> none  [dilated_valid(): lax.conv_general_dilated(widened[None], kernel, (1, 1), 'VALID', rhs_dila...]
  transfers between devices with their start and end apart: 28 -> 0, of which waited for: 15 -> 0; matrix products, arithmetic and copies ran while one was open for 4% -> 0% of each run, Pallas kernels for 0% -> 0%
where the time goes in v1:
time: 255 us
  Pallas kernels  249 us (98%)
  local copies, waits for them, and re-layouts  5.46 us (2%)
    pallas_call x1, Pallas kernels, body(): pl.pallas_call(functools.partial(kernel, rows, cols), out_shape=(jax.Shap...  249 us
    unnamed x5, local copies, waits for them, and re-layouts  5.46 us

profile of v1, /device:TPU:1, one launch (start us, length us, event | category | flops | bytes accessed | tf_op | source)
XLA Modules:
  0.0 254.6 jit_solution(6737714277043734603)
XLA Ops:
  0.6 248.5 %shard_map.67 = (bf16[2048,128]{1,0:T(8,128)(2,1)}, f32[3,1152,128]{2,1,0:T(8,128)}, f32[3,128,128]{2,1,0:T(8,128)}) custom-call(bf16[2048,128]{1,0:T(8,128)(2,1)} %bitcast.8, bf16[2048,128]{1,0:T(8,128)(2,1)} %bitcast.9, bf16[3,1152,128]{2,1,0:T(8,128)(2,1)} %bitcast.6, bf16[3,128,128]{2,1,0:T(8,128)(2,1)} %refs_3_.1), custom_call_target="tpu_custom_call" | custom-call | tf_op jit(solution)/shard_map/pallas_call | solution.py:673
  249.2 1.9 copy.10
  251.0 0.0 copy-start
  251.0 2.9 %copy.11 = f32[3,3,3,128,128]{4,3,2,1,0:T(8,128)} copy(f32[3,3,3,128,128]{4,3,2,1,0:T(8,128)} %bitcast.5) | data formatting | bytes 3538944
  254.0 0.0 copy-done
  254.0 0.7 copy.12
Async XLA Ops:
  251.0 2.9 %copy-start = (f32[3,128,128]{2,1,0:T(8,128)S(1)}, f32[3,128,128]{2,1,0:T(8,128)}, u32[]{:S(2)}) copy-start(f32[3,128,128]{2,1,0:T(8,128)} %get-tuple-element.14) | copy-start | bytes 589828

commit v2 on v1

--- a/solution.py
+++ b/solution.py
@@ -12,8 +12,10 @@
 F32 = jnp.float32
 ROWS, COLS, CH, MARGIN = 64, 32, 128, 8
 CELLS = ROWS * COLS
+CORNER = 16
+TALL = ROWS + 2 * CORNER
 HIGH, WIDE = ROWS + 2 * MARGIN, COLS + 2 * MARGIN
-STEP = 8
+STEP = 32
 CHUNK = STEP * COLS
 CHUNKS = ROWS // STEP
 TAPS = 9
@@ -21,8 +23,11 @@
 SLOPE_C = 0.7978845608028654
 CUBIC = 0.044715
 MOVES = ((0, -1), (0, 1), (-1, 0), (1, 0), (-1, -1), (-1, 1), (1, -1), (1, 1))
-GROUPS = ((2, 1), (0,))
+GROUPS = ((2, 1, 0),)
 BLOCK_ROWS = (TAPS + 1) * CH
+PIECES = 4
+EARLY = 4
+CONV_ROWS = BLOCKS * TAPS * CH
 
 
 def gelu_parts(v):
@@ -314,15 +319,15 @@
 
 
 def kernel(rows, cols, *refs):
-    (contact, cotangent, conv_w, proj_w, out_map, out_conv, out_proj,
-     own, grad, wf, wb, pw, hid, hslope, mid, slope, sh, wide, left, right, pack, mir, flat, acc, accp,
-     hsend, hrecv, msend, mrecv, mloc, loc) = refs[:31]
+    (contact, cotangent, conv_w, proj_w, out_map, out_sum,
+     own, grad, wf, wb, pw, hid, hslope, mid, slope, sh, wide, rim, left, right, pack, mir, flat, acc, accp,
+     hsend, hrecv, passing, msend, mrecv, psend, precv, mloc, loc) = refs[:34]
     p = Place(rows, cols)
     sent = Sent()
-    per = (len(refs) - 31) // len(GROUPS)
+    per = (len(refs) - 34) // len(GROUPS)
     reduces = []
     for index, blocks in enumerate(GROUPS):
-        start = 31 + index * per
+        start = 34 + index * per
         reduces.append(Reduce(len(blocks) * BLOCK_ROWS, p, sent, refs[start : start + per]))
 
     barrier = pltpu.get_barrier_semaphore()
@@ -345,10 +350,13 @@
         there = p.inside(dr, dc)
         pl.when(there)(functools.partial(greet, (p.r + dr, p.c + dc)))
         count = count + there.astype(jnp.int32)
-    apart = p.q != p.r
+    apart, turned, swapped = p.q != p.r, p.x != p.y, p.zh != p.zl
     for h in range(2):
         pl.when(apart)(functools.partial(greet, (p.q, 2 * p.r + h)))
-        count = count + apart.astype(jnp.int32)
+        pl.when(swapped)(functools.partial(greet, (p.zh * p.side + p.y, p.zl * 2 * p.side + 2 * p.x + h)))
+        count = count + apart.astype(jnp.int32) + swapped.astype(jnp.int32)
+    pl.when(turned)(functools.partial(greet, (p.zl * p.side + p.x, p.zh * 2 * p.side + 2 * p.y + p.k)))
+    count = count + turned.astype(jnp.int32)
 
     loads = [
         pltpu.make_async_copy(contact, own, loc.at[0]),
@@ -361,34 +369,70 @@
     pl.semaphore_wait(barrier, count)
 
     half = CELLS // 2
-
-    def mirror_copies(turn, source, h):
-        stays = (p.q == p.r) & (p.k == h)
-        src = source.at[pl.ds(h * half, half)]
-        dst = mir.at[turn, p.k]
-        there = remote(src, dst, msend.at[turn, h], mrecv.at[turn, p.k], (p.q, 2 * p.r + h))
-        here = pltpu.make_async_copy(src, dst, mloc.at[turn])
-        return stays, there, here
-
-    def mirror_start(turn, source, h):
-        stays, there, here = mirror_copies(turn, source, h)
-        sent.start(jnp.logical_not(stays), there)
-        pl.when(stays)(here.start)
+    piece = half // PIECES
+    by_relay = (p.x != p.y) & (p.zh != p.zl)
+    mirrored = (p.q, 2 * p.r)
+    relay = (p.zl * p.side + p.x, p.zh * 2 * p.side + 2 * p.y + p.k)
+    beyond = (p.zh * p.side + p.y, p.zl * 2 * p.side + 2 * p.x)
+    every = [(h, n) for n in range(PIECES) for h in range(2)]
+    odd = [(h, n) for h, n in every if n % 2 == 1]
+
+    def part_of(n):
+        return pl.ds(n * piece, piece)
+
+    def direct(turn, source, h, n):
+        src = source.at[pl.ds(h * half + n * piece, piece)]
+        dst = mir.at[turn, p.k, part_of(n)]
+        device = (mirrored[0], mirrored[1] + h)
+        return remote(src, dst, msend.at[turn, h, n], mrecv.at[turn, p.k, n], device)
+
+    def staying(turn, source, n):
+        src = source.at[pl.ds(p.k * half + n * piece, piece)]
+        return pltpu.make_async_copy(src, mir.at[turn, p.k, part_of(n)], mloc.at[turn, n])
+
+    def to_relay(turn, source, h, n):
+        src = source.at[pl.ds(h * half + n * piece, piece)]
+        return remote(src, passing.at[turn, h, part_of(n)], msend.at[turn, h, n], precv.at[turn, h, n], relay)
+
+    def from_relay(turn, h, n):
+        dst = mir.at[turn, p.k, part_of(n)]
+        device = (beyond[0], beyond[1] + h)
+        return remote(passing.at[turn, h, part_of(n)], dst, psend.at[turn, h, n], mrecv.at[turn, p.k, n], device)
+
+    same = p.q == p.r
+
+    def mirror_first(turn, source):
+        for h, n in odd:
+            sent.start(by_relay, to_relay(turn, source, h, n))
+
+    def mirror_direct(turn, source, pieces):
+        for h, n in pieces:
+            stays = same & (p.k == h)
+            goes = jnp.logical_not(stays)
+            if n % 2 == 1:
+                goes = goes & jnp.logical_not(by_relay)
+            sent.start(goes, direct(turn, source, h, n))
+            pl.when(stays)(staying(turn, source, n).start)
+
+    def mirror_forward(turn, source):
+        for h, n in odd:
+            pl.when(by_relay)(to_relay(turn, source, h, n).wait_recv)
+            sent.start(by_relay, from_relay(turn, h, n))
 
     def mirror_wait(turn, source):
-        for h in range(2):
-            stays = (p.q == p.r) & (p.k == h)
-            dst = mir.at[turn, h]
-            src = source.at[pl.ds(0, half)]
-            there = remote(src, dst, msend.at[turn, h], mrecv.at[turn, h], (p.q, 2 * p.r + h))
-            here = pltpu.make_async_copy(src, dst, mloc.at[turn])
-            pl.when(jnp.logical_not(stays))(there.wait_recv)
-            pl.when(stays)(here.wait)
+        for h, n in every:
+            stays = same & (p.k == h)
+            arrives = remote(mir.at[turn, h, part_of(n)], mir.at[turn, h, part_of(n)], msend.at[turn, h, n],
+                             mrecv.at[turn, h, n], (mirrored[0], mirrored[1] + h))
+            pl.when(jnp.logical_not(stays))(arrives.wait_recv)
+            pl.when(stays)(staying(turn, source, n).wait)
 
     def mirror_spread(turn):
+        steps = half // CHUNK
+
         def body(i, _):
             flat[pl.ds(pl.multiple_of(i * CHUNK, CHUNK), CHUNK), :] = mir[
-                turn, i // 4, pl.ds(pl.multiple_of((i % 4) * CHUNK, CHUNK), CHUNK), :
+                turn, i // steps, pl.ds(pl.multiple_of((i % steps) * CHUNK, CHUNK), CHUNK), :
             ].astype(F32)
             return 0
 
@@ -398,31 +442,28 @@
         base = (chunk // (COLS // STEP)) * half + (chunk % (COLS // STEP)) * STEP
         return jnp.concatenate([flat[pl.ds(base + j, COLS, stride=COLS), :] for j in range(STEP)], axis=0)
 
-    for h in range(2):
-        mirror_start(0, contact, h)
+    mirror_first(0, contact)
+    mirror_direct(0, contact, every)
+    mirror_forward(0, contact)
 
     zero = functools.partial(jnp.zeros, dtype=BF)
-    corner = MARGIN * MARGIN
-    low, side_rows = (MARGIN + ROWS) * MARGIN, ROWS * MARGIN
-
-    def fill(dr, dc, ref, start, size):
+
+    def fill(dr, dc, ref, at, shape):
         @pl.when(jnp.logical_not(p.inside(dr, dc)))
         def _():
             def body(e, _):
-                if ref is sh:
-                    sh[e, 1, pl.ds(start, size), :] = zero((size, CH))
-                else:
-                    ref[e, pl.ds(start, size), :] = zero((size, CH))
+                ref[(e, *at)] = zero(shape)
                 return 0
 
             lax.fori_loop(0, 2 * BLOCKS, body, 0)
 
-    fill(-1, 0, sh, 0, MARGIN * COLS)
-    fill(1, 0, sh, (MARGIN + ROWS) * COLS, MARGIN * COLS)
+    strip = MARGIN * COLS
+    fill(-1, 0, sh, (1, pl.ds(0, strip)), (strip, CH))
+    fill(1, 0, sh, (1, pl.ds((MARGIN + ROWS) * COLS, strip)), (strip, CH))
     for dc, ref in ((-1, left), (1, right)):
-        fill(-1, dc, ref, 0, corner)
-        fill(0, dc, ref, corner, side_rows)
-        fill(1, dc, ref, low, corner)
+        fill(-1, dc, ref, (slice(None), pl.ds(0, CORNER)), (MARGIN, CORNER, CH))
+        fill(0, dc, ref, (slice(None), pl.ds(CORNER, ROWS)), (MARGIN, ROWS, CH))
+        fill(1, dc, ref, (slice(None), pl.ds(CORNER + ROWS, CORNER)), (MARGIN, CORNER, CH))
 
     loads[2].wait()
     loads[3].wait()
@@ -442,29 +483,35 @@
 
     def put_center(e, chunk, values):
         rounded = values.astype(BF)
-        sh[e, 1, pl.ds(pl.multiple_of(chunk * CHUNK + MARGIN * COLS, CHUNK), CHUNK), :] = rounded
+        sh[e, 1, pl.ds(pl.multiple_of(chunk * CHUNK + MARGIN * COLS, MARGIN * COLS), CHUNK), :] = rounded
         cube = values.reshape(STEP, COLS, CH)
         wide[pl.ds(chunk * STEP + MARGIN, STEP), MARGIN : MARGIN + COLS, :] = cube
         edge = STEP * MARGIN
         at = pl.ds(pl.multiple_of(chunk * edge, edge), edge)
-        pack[e, 0, at, :] = cube[:, :MARGIN, :].reshape(edge, CH).astype(BF)
-        pack[e, 1, at, :] = cube[:, COLS - MARGIN :, :].reshape(edge, CH).astype(BF)
+        rim[0, at, :] = cube[:, :MARGIN, :].reshape(edge, CH)
+        rim[1, at, :] = cube[:, COLS - MARGIN :, :].reshape(edge, CH)
 
     def halo_copy(e, d, index):
         dr, dc = MOVES[index]
         strip = d * COLS
+        side = (dc + 1) // 2
+        margin = right if dc < 0 else left
         if dr == 0:
-            src, dst = pack.at[e, (dc + 1) // 2], (right if dc < 0 else left).at[e, pl.ds(corner, side_rows)]
+            src = pack.at[e, side, pl.ds(0, d)]
+            dst = margin.at[e, pl.ds(0, d), pl.ds(CORNER, ROWS)]
         elif dc == 0:
             start, end = (MARGIN, MARGIN + ROWS) if dr < 0 else (MARGIN + ROWS - d, MARGIN - d)
             src = sh.at[e, 1, pl.ds(start * COLS, strip)]
             dst = sh.at[e, 1, pl.ds(end * COLS, strip)]
         else:
-            src = pack.at[e, (dc + 1) // 2, pl.ds(0 if dr < 0 else side_rows - corner, corner)]
-            dst = (right if dc < 0 else left).at[e, pl.ds(low if dr < 0 else 0, corner)]
+            src = pack.at[e, side, pl.ds(0, d), pl.ds(0 if dr < 0 else ROWS - CORNER, CORNER)]
+            dst = margin.at[e, pl.ds(0, d), pl.ds(CORNER + ROWS if dr < 0 else 0, CORNER)]
         return remote(src, dst, hsend.at[e, index], hrecv.at[e, index], (p.r + dr, p.c + dc))
 
     def halo_start(e, d):
+        for j in range(d):
+            pack[e, 0, j, :, :] = rim[0, pl.ds(j, ROWS, stride=MARGIN), :].astype(BF)
+            pack[e, 1, j, :, :] = rim[1, pl.ds(MARGIN - d + j, ROWS, stride=MARGIN), :].astype(BF)
         for index, (dr, dc) in enumerate(MOVES):
             sent.start(p.inside(dr, dc), halo_copy(e, d, index))
 
@@ -473,24 +520,22 @@
             pl.when(p.inside(-dr, -dc))(halo_copy(e, d, index).wait_recv)
 
     def halo_build(e, d):
-        def sides(i, _):
-            at = pl.ds(pl.multiple_of(i * corner, corner), corner)
-            to = pl.ds(i * MARGIN, MARGIN)
-            wide[to, :MARGIN, :] = left[e, at, :].astype(F32).reshape(MARGIN, MARGIN, CH)
-            wide[to, MARGIN + COLS :, :] = right[e, at, :].astype(F32).reshape(MARGIN, MARGIN, CH)
-            return 0
-
-        lax.fori_loop(0, HIGH // MARGIN, sides, 0)
+        for j in range(d):
+            inner = CORNER - MARGIN
+            rim[0, pl.ds(MARGIN - d + j, HIGH, stride=MARGIN), :] = left[e, j, :, :].astype(F32)[inner : inner + HIGH]
+            rim[1, pl.ds(j, HIGH, stride=MARGIN), :] = right[e, j, :, :].astype(F32)[inner : inner + HIGH]
+        wide[:, :MARGIN, :] = rim[0].reshape(HIGH, MARGIN, CH)
+        wide[:, MARGIN + COLS :, :] = rim[1].reshape(HIGH, MARGIN, CH)
         for start in (MARGIN - d, MARGIN + ROWS):
-            strip = sh[e, 1, start * COLS : (start + d) * COLS, :].astype(F32)
-            wide[start : start + d, MARGIN : MARGIN + COLS, :] = strip.reshape(d, COLS, CH)
+            edge = sh[e, 1, start * COLS : (start + d) * COLS, :].astype(F32)
+            wide[start : start + d, MARGIN : MARGIN + COLS, :] = edge.reshape(d, COLS, CH)
 
         def shift(i, _):
             first = MARGIN - d + 4 * i
             for b in (0, 2):
                 begin = MARGIN + (b - 1) * d
-                cube = wide[pl.ds(first, 4), begin : begin + COLS, :]
-                sh[e, b, pl.ds(pl.multiple_of(first * COLS, 2 * COLS), 4 * COLS), :] = cube.reshape(4 * COLS, CH).astype(BF)
+                moved = wide[pl.ds(first, 4), begin : begin + COLS, :]
+                sh[e, b, pl.ds(pl.multiple_of(first * COLS, 2 * COLS), 4 * COLS), :] = moved.reshape(4 * COLS, CH).astype(BF)
             return 0
 
         lax.fori_loop(0, (ROWS + 2 * d) // 4, shift, 0)
@@ -546,10 +591,10 @@
 
         each_chunk(forward)
 
-    queue = []
+    queues = []
 
     def advance(steps):
-        for _ in range(steps):
+        for queue in queues * steps:
             if queue:
                 queue.pop(0)()
 
@@ -577,13 +622,12 @@
         d = 2 ** (k + 1)
         e = 2 * BLOCKS - 1 - k
         halo_start(e, d)
-        advance(1)
         acc[...] = jnp.zeros_like(acc)
         accp[...] = jnp.zeros_like(accp)
 
         def weights(chunk, k=k, d=d, e=e):
             at = cells(chunk)
-            back = sh[e, 1, pl.ds(pl.multiple_of(chunk * CHUNK + MARGIN * COLS, CHUNK), CHUNK), :]
+            back = sh[e, 1, pl.ds(pl.multiple_of(chunk * CHUNK + MARGIN * COLS, MARGIN * COLS), CHUNK), :]
             acc[...] += dot_tn(back, windows(k, d, chunk))
             accp[...] += dot_tn(mid[k, at, :], grad[at, :])
 
@@ -595,11 +639,10 @@
             red.src[base + tap * CH : base + (tap + 1) * CH, :] = acc[:, tap * CH : (tap + 1) * CH].T.astype(BF)
         red.src[base + TAPS * CH : base + BLOCK_ROWS, :] = accp[...].astype(BF)
         if k == GROUPS[group][-1]:
-            queue.extend(phases(red))
+            queues.append(phases(red))
         advance(1)
         halo_wait(e, d)
         halo_build(e, d)
-        advance(1)
 
         def backward(chunk, k=k, d=d, e=e):
             at = cells(chunk)
@@ -610,18 +653,21 @@
                 put_center(e + 1, chunk, dot_nt(new, pw[k - 1]) * slope[k - 1, at, :])
 
         each_chunk(backward)
-
-    for h in range(2):
-        mirror_start(1, grad, h)
-    while queue:
         advance(1)
-    scale = 1.0 / (rows * ROWS)
+
+    mirror_first(1, grad)
+    mirror_direct(1, grad, every[:EARLY])
+    mirror_forward(1, grad)
+    advance(1)
+    mirror_direct(1, grad, every[EARLY:])
+    while any(queues):
+        advance(1)
     for group, blocks in enumerate(GROUPS):
         for place, k in enumerate(blocks):
             base = place * BLOCK_ROWS
             fin = reduces[group].fin
-            out_conv[k, :, :] = fin[base : base + TAPS * CH, :].astype(F32) * scale
-            out_proj[k, :, :] = fin[base + TAPS * CH : base + BLOCK_ROWS, :].astype(F32) * scale
+            out_sum[k * TAPS * CH : (k + 1) * TAPS * CH, :] = fin[base : base + TAPS * CH, :]
+            out_sum[CONV_ROWS + k * CH : CONV_ROWS + (k + 1) * CH, :] = fin[base + TAPS * CH : base + BLOCK_ROWS, :]
     mirror_wait(1, grad)
     mirror_spread(1)
 
@@ -652,33 +698,38 @@
         vmem((BLOCKS, CELLS, CH), F32),
         vmem((2 * BLOCKS, 3, HIGH * COLS, CH), BF),
         vmem((HIGH, WIDE, CH), F32),
-        vmem((2 * BLOCKS, HIGH * MARGIN, CH), BF),
-        vmem((2 * BLOCKS, HIGH * MARGIN, CH), BF),
-        vmem((2 * BLOCKS, 2, ROWS * MARGIN, CH), BF),
+        vmem((2, HIGH * MARGIN, CH), F32),
+        vmem((2 * BLOCKS, MARGIN, TALL, CH), BF),
+        vmem((2 * BLOCKS, MARGIN, TALL, CH), BF),
+        vmem((2 * BLOCKS, 2, MARGIN, ROWS, CH), BF),
         vmem((2, 2, CELLS // 2, CH), BF),
         vmem((CELLS, CH), F32),
         vmem((CH, TAPS * CH), F32),
         vmem((CH, CH), F32),
         dma((2 * BLOCKS, 8)),
         dma((2 * BLOCKS, 8)),
-        dma((2, 2)),
-        dma((2, 2)),
-        dma((2,)),
+        vmem((2, 2, CELLS // 2, CH), BF),
+        dma((2, 2, PIECES)),
+        dma((2, 2, PIECES)),
+        dma((2, 2, PIECES)),
+        dma((2, 2, PIECES)),
+        dma((2, PIECES)),
         dma((4,)),
     ]
     for blocks in GROUPS:
         scratch += Reduce.scratch(len(blocks) * BLOCK_ROWS, side, depth)
 
+    scale = 1.0 / (rows * ROWS)
+
     def body(contact_map, cotangent, conv_weight, proj_weight):
-        out_map, out_conv, out_proj = pl.pallas_call(
+        out_map, out_sum = pl.pallas_call(
             functools.partial(kernel, rows, cols),
             out_shape=(
                 jax.ShapeDtypeStruct((CELLS, CH), BF),
-                jax.ShapeDtypeStruct((BLOCKS, TAPS * CH, CH), F32),
-                jax.ShapeDtypeStruct((BLOCKS, CH, CH), F32),
+                jax.ShapeDtypeStruct((BLOCKS * BLOCK_ROWS, CH), BF),
             ),
             in_specs=[pl.BlockSpec(memory_space=pl.ANY)] * 4,
-            out_specs=(pl.BlockSpec(memory_space=pltpu.VMEM),) * 3,
+            out_specs=(pl.BlockSpec(memory_space=pltpu.VMEM),) * 2,
             scratch_shapes=scratch,
             compiler_params=pltpu.CompilerParams(
                 collective_id=0, has_side_effects=True, vmem_limit_bytes=56 * 1024 * 1024
@@ -691,8 +742,8 @@
         )
         return (
             out_map.reshape(ROWS, COLS, CH),
-            out_conv.reshape(BLOCKS, 3, 3, CH, CH),
-            out_proj,
+            (out_sum[:CONV_ROWS].astype(F32) * scale).reshape(BLOCKS, 3, 3, CH, CH),
+            (out_sum[CONV_ROWS:].astype(F32) * scale).reshape(BLOCKS, CH, CH),
         )
 
     in_specs = (P("row", "col", None), P("row", "col", None), P(), P())

time: 255 us -> 203 us (0.80)
  Pallas kernels: 249 us -> 195 us
  local copies, waits for them, and re-layouts: 5.46 us -> 0.8 us
  other arithmetic: 0 us -> 4.13 us
    pallas_call x1, Pallas kernels: 249 us -> 195 us  [body(): pl.pallas_call(functools.partial(kernel, rows, cols), out_shape=(jax.Shap...]
    unnamed x5 -> x3, local copies, waits for them, and re-layouts: 5.46 us -> 0.8 us
    mul x0 -> x2, other arithmetic: none -> 4.13 us  [the longest x1 2.49 us: body(): out_sum[:CONV_ROWS].astype(F32) * scale]
where the time goes in v2:
time: 203 us; the launch traced here: 200 us
  Pallas kernels  195 us (96%)
  other arithmetic  4.13 us (2%)
    pallas_call x1, Pallas kernels, body(): pl.pallas_call(functools.partial(kernel, rows, cols), out_shape=(jax.Shap...  195 us

profile of v2, /device:TPU:1, one launch (start us, length us, event | category | flops | bytes accessed | tf_op | source)
XLA Modules:
  0.0 200.2 jit_solution(623673827924459884)
XLA Ops:
  0.6 194.6 %shard_map.67 = (bf16[2048,128]{1,0:T(8,128)(2,1)}, bf16[3840,128]{1,0:T(8,128)(2,1)}) custom-call(bf16[2048,128]{1,0:T(8,128)(2,1)} %bitcast.9, bf16[2048,128]{1,0:T(8,128)(2,1)} %bitcast.10, bf16[3,1152,128]{2,1,0:T(8,128)(2,1)} %bitcast.7, bf16[3,128,128]{2,1,0:T(8,128)(2,1)} %refs_3_.1), custom_call_target="tpu_custom_call" | custom-call | tf_op jit(solution)/shard_map/pallas_call | solution.py:725
  195.2 0.0 copy-start
  195.2 1.6 convert_multiply_fusion.1
  196.9 2.5 %convert_multiply_fusion = f32[3456,128]{1,0:T(8,128)} fusion(bf16[3840,128]{1,0:T(8,128)(2,1)} %get-tuple-element.6), kind=kLoop, calls=%fused_computation | loop fusion | flops 884736 | bytes 2654208 | tf_op jit(solution)/shard_map/mul | solution.py:745
  199.4 0.0 copy-done
  199.4 0.8 copy.8
Async XLA Ops:
  195.2 4.1 %copy-start = (bf16[2048,128]{1,0:T(8,128)(2,1)S(1)}, bf16[2048,128]{1,0:T(8,128)(2,1)}, u32[]{:S(2)}) copy-start(bf16[2048,128]{1,0:T(8,128)(2,1)} %get-tuple-element.5) | copy-start | bytes 1572868

commit v3 on v2

--- a/solution.py
+++ b/solution.py
@@ -22,7 +22,7 @@
 BLOCKS = 3
 SLOPE_C = 0.7978845608028654
 CUBIC = 0.044715
-MOVES = ((0, -1), (0, 1), (-1, 0), (1, 0), (-1, -1), (-1, 1), (1, -1), (1, 1))
+MOVES = ((-1, -1), (-1, 1), (1, -1), (1, 1), (0, -1), (0, 1), (-1, 0), (1, 0))
 GROUPS = ((2, 1, 0),)
 BLOCK_ROWS = (TAPS + 1) * CH
 PIECES = 4

time: 203 us -> 199 us (0.980)
  Pallas kernels: 195 us -> 191 us
    pallas_call x1, Pallas kernels: 195 us -> 191 us  [body(): pl.pallas_call(functools.partial(kernel, rows, cols), out_shape=(jax.Shap...]
where the time goes in v3:
time: 199 us; the launch traced here: 196 us
  Pallas kernels  191 us (96%)
  other arithmetic  4.13 us (2%)
    pallas_call x1, Pallas kernels, body(): pl.pallas_call(functools.partial(kernel, rows, cols), out_shape=(jax.Shap...  191 us

profile of v3, /device:TPU:1, one launch (start us, length us, event | category | flops | bytes accessed | tf_op | source)
XLA Modules:
  0.0 196.3 jit_solution(5288572971887382091)
XLA Ops:
  0.6 190.7 %shard_map.67 = (bf16[2048,128]{1,0:T(8,128)(2,1)}, bf16[3840,128]{1,0:T(8,128)(2,1)}) custom-call(bf16[2048,128]{1,0:T(8,128)(2,1)} %bitcast.9, bf16[2048,128]{1,0:T(8,128)(2,1)} %bitcast.10, bf16[3,1152,128]{2,1,0:T(8,128)(2,1)} %bitcast.7, bf16[3,128,128]{2,1,0:T(8,128)(2,1)} %refs_3_.1), custom_call_target="tpu_custom_call" | custom-call | tf_op jit(solution)/shard_map/pallas_call | solution.py:725
  191.4 0.0 copy-start
  191.4 1.6 convert_multiply_fusion.1
  193.0 2.5 %convert_multiply_fusion = f32[3456,128]{1,0:T(8,128)} fusion(bf16[3840,128]{1,0:T(8,128)(2,1)} %get-tuple-element.6), kind=kLoop, calls=%fused_computation | loop fusion | flops 884736 | bytes 2654208 | tf_op jit(solution)/shard_map/mul | solution.py:745
  195.5 0.0 copy-done
  195.5 0.8 copy.8
Async XLA Ops:
  191.4 4.1 %copy-start = (bf16[2048,128]{1,0:T(8,128)(2,1)S(1)}, bf16[2048,128]{1,0:T(8,128)(2,1)}, u32[]{:S(2)}) copy-start(bf16[2048,128]{1,0:T(8,128)(2,1)} %get-tuple-element.5) | copy-start | bytes 1572868

commit v4 on v3

--- a/solution.py
+++ b/solution.py
@@ -660,22 +660,23 @@
     mirror_forward(1, grad)
     advance(1)
     mirror_direct(1, grad, every[EARLY:])
-    while any(queues):
+    while any(len(queue) > 1 for queue in queues):
         advance(1)
+    mirror_wait(1, grad)
+    mirror_spread(1)
+
+    def last(chunk):
+        at = cells(chunk)
+        out_map[at, :] = (0.5 * (grad[at, :].astype(F32) + mirror_rows(chunk))).astype(BF)
+
+    each_chunk(last)
+    advance(1)
     for group, blocks in enumerate(GROUPS):
         for place, k in enumerate(blocks):
             base = place * BLOCK_ROWS
             fin = reduces[group].fin
             out_sum[k * TAPS * CH : (k + 1) * TAPS * CH, :] = fin[base : base + TAPS * CH, :]
             out_sum[CONV_ROWS + k * CH : CONV_ROWS + (k + 1) * CH, :] = fin[base + TAPS * CH : base + BLOCK_ROWS, :]
-    mirror_wait(1, grad)
-    mirror_spread(1)
-
-    def last(chunk):
-        at = cells(chunk)
-        out_map[at, :] = (0.5 * (grad[at, :].astype(F32) + mirror_rows(chunk))).astype(BF)
-
-    each_chunk(last)
     sent.finish()
     for red in reduces:
         red.finish_sends()

time: 199 us -> 198 us (level)
  no operation moved by 1% of the time
where the time goes in v4:
time: 198 us; the launch traced here: 196 us
  Pallas kernels  190 us (96%)
  other arithmetic  4.13 us (2%)
    pallas_call x1, Pallas kernels, body(): pl.pallas_call(functools.partial(kernel, rows, cols), out_shape=(jax.Shap...  190 us

profile of v4, /device:TPU:1, one launch (start us, length us, event | category | flops | bytes accessed | tf_op | source)
XLA Modules:
  0.0 195.5 jit_solution(2795044886601744674)
XLA Ops:
  0.6 190.0 %shard_map.67 = (bf16[2048,128]{1,0:T(8,128)(2,1)}, bf16[3840,128]{1,0:T(8,128)(2,1)}) custom-call(bf16[2048,128]{1,0:T(8,128)(2,1)} %bitcast.9, bf16[2048,128]{1,0:T(8,128)(2,1)} %bitcast.10, bf16[3,1152,128]{2,1,0:T(8,128)(2,1)} %bitcast.7, bf16[3,128,128]{2,1,0:T(8,128)(2,1)} %refs_3_.1), custom_call_target="tpu_custom_call" | custom-call | tf_op jit(solution)/shard_map/pallas_call | solution.py:726
  190.6 0.0 copy-start
  190.6 1.6 convert_multiply_fusion.1
  192.3 2.5 %convert_multiply_fusion = f32[3456,128]{1,0:T(8,128)} fusion(bf16[3840,128]{1,0:T(8,128)(2,1)} %get-tuple-element.6), kind=kLoop, calls=%fused_computation | loop fusion | flops 884736 | bytes 2654208 | tf_op jit(solution)/shard_map/mul | solution.py:746
  194.7 0.0 copy-done
  194.7 0.8 copy.8
Async XLA Ops:
  190.6 4.1 %copy-start = (bf16[2048,128]{1,0:T(8,128)(2,1)S(1)}, bf16[2048,128]{1,0:T(8,128)(2,1)}, u32[]{:S(2)}) copy-start(bf16[2048,128]{1,0:T(8,128)(2,1)} %get-tuple-element.5) | copy-start | bytes 1572868
